TPU v7x, 32 devices: a whole 2x2x4 slice. The times are simulated.
32 devices in a mesh: ctx: 2 (over x), tp: 4 (over z), dp: 4 (over y, core).
Axes of the slice: x: 2, y: 2, z: 4, core: 2. Of those that a mesh axis runs over, the one named last changes fastest.
Arguments:
- trailing_questions: bfloat16 [1024, 8192], P(('dp', 'ctx'), 'tp'), parts along dimension 0, may hold values from -6 to 6
- output_gradient: bfloat16 [1024, 8192], P(('dp', 'ctx'), 'tp'), parts along dimension 0, may hold values from -6 to 6
- tail_row_key: bfloat16 [1024, 1024], P(('dp', 'ctx'), 'tp'), parts along dimension 0, may hold values from -6 to 6
- tail_row_value: bfloat16 [1024, 1024], P(('dp', 'ctx'), 'tp'), parts along dimension 0, may hold values from -6 to 6
- passage_key_cache: bfloat16 [2048, 1024], P(('dp', 'ctx'), 'tp'), parts along dimension 0, may hold values from -6 to 6
- passage_value_cache: bfloat16 [2048, 1024], P(('dp', 'ctx'), 'tp'), parts along dimension 0, may hold values from -6 to 6
- row_list: int32 [1024], P(('dp', 'ctx')), parts along dimension 0, may hold values from 0 to 1, as said below
- read_owner: int32 [8, 24], P(('dp', 'ctx')), parts along dimension 0, may hold values from 0 to 1, as said below
- read_tile: int32 [8, 24], P(('dp', 'ctx')), parts along dimension 0, may hold values from 0 to 1
- read_list: int32 [8, 24], P(('dp', 'ctx')), parts along dimension 0, may hold values from 0 to 1
- read_count: int32 [8], P(('dp', 'ctx')), parts along dimension 0, may hold values from 12 to 24, as said below
Outputs:
- grad_query: bfloat16 [1024, 8192], P(('dp', 'ctx'), 'tp'), parts along dimension 0
- grad_tail_key: bfloat16 [1024, 1024], P(('dp', 'ctx'), 'tp'), parts along dimension 0
- grad_tail_value: bfloat16 [1024, 1024], P(('dp', 'ctx'), 'tp'), parts along dimension 0
- grad_key_cache: float32 [2048, 1024], P(('dp', 'ctx'), 'tp'), parts along dimension 0
- grad_value_cache: float32 [2048, 1024], P(('dp', 'ctx'), 'tp'), parts along dimension 0
There are 4 independent parts, one for each index of `dp`. A program takes and returns all parts, laid end to end along the dimension named above; each array names one. Nothing has to cross between parts.
Inputs may be any that keep to these rules, and one draw needn't show every extreme that they name: `row_list`: on each reader's 128 rows the list number is 0 on a first run and 1 on the rest; both runs are nonempty. `read_owner`: a reader names one owner at most 12 times, and every reader names some owner exactly 12 times. `read_count`: some reader has all 24 reads live.
All inputs are finite; a program needn't handle non-finite values.
Results may differ from a plain program's by a relative error of at most 0.012.
Values may be sent and summed in bfloat16 or wider, within the bound.
No kernel may reach another device: no remote copies, remote signals or barrier semaphores. Data moves between devices by JAX's collectives and lax.ppermute only.
A program may use at most 64 MiB of HBM per device.

v0:
```python
import functools
import math

import jax
import jax.numpy as jnp
from jax import lax
from jax.experimental import pallas as pl
from jax.experimental.pallas import tpu as pltpu
from jax.sharding import PartitionSpec as P

WIDTH = 128
TILE = 128
PAIR = 2 * WIDTH
NEAR_OUTS = 12
NEG = -1e30
SCALE = 1.0 / math.sqrt(WIDTH)
SCALE2 = SCALE * math.log2(math.e)
F32 = jnp.float32
BF16 = jnp.bfloat16


def dot_nt(a, b):
    return lax.dot_general(a, b, (((1,), (1,)), ((), ())), preferred_element_type=F32)


def dot_nn(a, b):
    return lax.dot_general(a, b, (((1,), (0,)), ((), ())), preferred_element_type=F32)


def dot_tn(a, b):
    return lax.dot_general(a, b, (((0,), (0,)), ((), ())), preferred_element_type=F32)


def repeat(steps, unroll, step):
    if unroll:
        for i in range(steps):
            step(i)
    else:

        def one(i, carry):
            step(i)
            return carry

        lax.fori_loop(0, steps, one, 0)


def added(steps, unroll, step, total_ref):
    if unroll:
        return functools.reduce(jnp.add, [step(i) for i in range(steps)])
    (total_ref,) = total_ref
    total_ref[...] = jnp.zeros_like(total_ref)

    def one(i):
        total_ref[...] += step(i)

    repeat(steps, unroll, one)
    return total_ref[...]


def columns(i, width):
    if isinstance(i, int):
        return pl.ds(i * width, width)
    return pl.ds(pl.multiple_of(i * width, width), width)


def pair_rows(ref, i):
    block = ref[:, columns(i, PAIR)]
    return jnp.concatenate([block[:, :WIDTH], block[:, WIDTH:]], axis=0)


def stacked_rows(ref, head, group):
    first = head * group
    return jnp.concatenate(
        [ref[:, (first + g) * WIDTH : (first + g + 1) * WIDTH] for g in range(group)], axis=0
    )


def twice(row):
    return jnp.concatenate([row, row], axis=1)


def tile_bias(table, first, tiles):
    return [twice(table[first + t : first + t + 1, :]) for t in range(tiles)]


def add_tiles(scores, biases):
    parts = [
        scores[t * TILE : (t + 1) * TILE, :] * SCALE2 + bias for t, bias in enumerate(biases)
    ]
    return parts[0] if len(parts) == 1 else jnp.concatenate(parts, axis=0)


def tail_bias(row_list):
    rows = row_list.shape[1]
    cut = jnp.sum((row_list == 0).astype(jnp.int32), axis=1, keepdims=True)
    key_at = lax.broadcasted_iota(jnp.int32, (rows, rows), 0)
    row_at = lax.broadcasted_iota(jnp.int32, (rows, rows), 1)
    allowed = ((key_at < cut) == (row_at < cut)) & (key_at <= row_at)
    return twice(jnp.where(allowed, 0.0, NEG).astype(F32))


def is_odd():
    return lax.rem(lax.axis_index("dp"), 2) == 1


def value_part_late():
    return jnp.logical_and(jnp.logical_not(is_odd()), lax.axis_index("ctx") > 0)


def load_copies(ins, q_ref, g_ref, k_ref, v_ref, small_refs, sems):
    q_in, g_in, tk_in, tv_in, ok_in, ov_in, *small_ins = ins
    tail = tk_in.shape[0]
    moves = list(zip(small_ins, small_refs)) + [
        (tk_in, k_ref.at[:tail]), (ok_in, k_ref.at[tail:]), (q_in, q_ref),
        (tv_in, v_ref.at[:tail]), (ov_in, v_ref.at[tail:]), (g_in, g_ref),
    ]
    copies = [pltpu.make_async_copy(a, b, sems.at[i]) for i, (a, b) in enumerate(moves)]
    for copy in copies:
        copy.start()
    return copies


def raw_scores(q_ref, k_ref, head, i, per_head):
    cols = slice(head * WIDTH, (head + 1) * WIDTH)
    return dot_nt(k_ref[:, cols], pair_rows(q_ref, head * per_head + i))


def near_raw_work(q_ref, k_ref, p_ref):
    heads = k_ref.shape[1] // WIDTH
    per_head = q_ref.shape[1] // PAIR // heads
    for head in range(heads):
        for i in range(per_head):
            p_ref[head, :, columns(i, PAIR)] = raw_scores(q_ref, k_ref, head, i, per_head)


def near_key_work(
    ctx, own, raw_made, q_ref, k_ref, p_ref, stats_ref, table_ref,
    rl_ref, ro_ref, rt_ref, rs_ref, rc_ref,
):
    heads = k_ref.shape[1] // WIDTH
    per_head = q_ref.shape[1] // PAIR // heads
    reads = ro_ref.shape[1]
    slots = table_ref.shape[0]
    row_list = rl_ref[...]
    owner = ro_ref[...] - lax.axis_index("ctx")
    owner = jnp.where(owner < 0, owner + ctx, owner)
    wanted = owner * own + rt_ref[...]
    live = lax.broadcasted_iota(jnp.int32, (1, reads), 1) < rc_ref[0]
    wanted = jnp.where(live, wanted, -1)
    hit = lax.broadcasted_iota(jnp.int32, (slots, reads), 0) == wanted
    first = rs_ref[...] == 0
    count0 = jnp.sum(jnp.where(hit & first, 1.0, 0.0), axis=1, keepdims=True)
    count1 = jnp.sum(jnp.where(hit & jnp.logical_not(first), 1.0, 0.0), axis=1, keepdims=True)
    count = jnp.where(row_list == 0, count0, count1)
    table = jnp.where(count > 0.5, jnp.log2(jnp.maximum(count, 1.0)), NEG)
    table_ref[...] = table
    biases = [tail_bias(row_list)] + tile_bias(table, 0, own)
    for head in range(heads):
        for i in range(per_head):
            at = columns(head * per_head + i, PAIR)
            here = columns(i, PAIR)
            if raw_made:
                raw = p_ref[head, :, here]
            else:
                raw = raw_scores(q_ref, k_ref, head, i, per_head)
            s = add_tiles(raw, biases)
            top = jnp.max(s, axis=0, keepdims=True)
            p = jnp.exp2(s - top)
            p_ref[head, :, here] = p
            stats_ref[0:1, at] = top
            stats_ref[1:2, at] = jnp.sum(p, axis=0, keepdims=True)


def near_dprob_work(g_ref, v_ref, d_ref):
    heads = v_ref.shape[1] // WIDTH
    per_head = g_ref.shape[1] // PAIR // heads
    for head in range(heads):
        for i in range(per_head):
            d_ref[head, :, columns(i, PAIR)] = raw_scores(g_ref, v_ref, head, i, per_head)


def near_cross_work(p_ref, d_ref, stats_ref):
    heads, _, group_rows = p_ref.shape
    for head in range(heads):
        for i in range(group_rows // PAIR):
            here = columns(i, PAIR)
            cross = jnp.sum(p_ref[head, :, here] * d_ref[head, :, here], axis=0, keepdims=True)
            stats_ref[2:3, columns(head * group_rows // PAIR + i, PAIR)] = cross


def near_value_work(g_ref, v_ref, p_ref, d_ref, stats_ref):
    heads = v_ref.shape[1] // WIDTH
    per_head = g_ref.shape[1] // PAIR // heads
    for head in range(heads):
        cols = slice(head * WIDTH, (head + 1) * WIDTH)
        for i in range(per_head):
            pair = head * per_head + i
            here = columns(i, PAIR)
            d = dot_nt(v_ref[:, cols], pair_rows(g_ref, pair))
            d_ref[head, :, here] = d
            cross = jnp.sum(p_ref[head, :, here] * d, axis=0, keepdims=True)
            stats_ref[2:3, columns(pair, PAIR)] = cross


def near_kernel(ctx, early, *refs):
    ins, rest = refs[:10], refs[10 if early else 11 + NEAR_OUTS :]
    q_ref, g_ref, k_ref, v_ref, *small_refs = rest[:8]
    p_ref, d_ref, stats_ref, table_ref, sems = rest[8:]

    def load():
        copies = load_copies(ins, q_ref, g_ref, k_ref, v_ref, small_refs, sems)
        for copy in copies:
            copy.wait()

    if early:

        @pl.when(is_odd())
        def first_part():
            load()
            near_raw_work(q_ref, k_ref, p_ref)
            near_dprob_work(g_ref, v_ref, d_ref)

        return
    own = ins[4].shape[0] // TILE
    refs_of_keys = (q_ref, k_ref, p_ref, stats_ref, table_ref, *small_refs, refs[10])

    @pl.when(is_odd())
    def rest_of_it():
        near_key_work(ctx, own, True, *refs_of_keys)
        near_cross_work(p_ref, d_ref, stats_ref)

    @pl.when(jnp.logical_not(is_odd()))
    def key_part():
        load()
        near_key_work(ctx, own, False, *refs_of_keys)

    @pl.when(jnp.logical_not(jnp.logical_or(is_odd(), value_part_late())))
    def value_part():
        near_value_work(g_ref, v_ref, p_ref, d_ref, stats_ref)


def far_key_kernel(
    unroll, q_ref, g_ref, k_ref, stats_ref, table_ref, back_ref, p_ref, fin_ref, *total_ref
):
    far_tiles = k_ref.shape[0] // TILE
    heads = k_ref.shape[1] // WIDTH
    per_head = q_ref.shape[1] // PAIR // heads
    shifts, own_keys, _ = back_ref.shape
    biases = tile_bias(table_ref[...], own_keys // TILE, far_tiles)
    for head in range(heads):
        cols = slice(head * WIDTH, (head + 1) * WIDTH)

        def step(i):
            pair = head * per_head + i
            at = columns(pair, PAIR)
            here = columns(i, PAIR)
            s = add_tiles(dot_nt(k_ref[:, cols], pair_rows(q_ref, pair)), biases)
            near_top = stats_ref[0:1, at]
            top = jnp.maximum(near_top, jnp.max(s, axis=0, keepdims=True))
            p = jnp.exp2(s - top)
            fade = jnp.exp2(near_top - top)
            inverse = 1.0 / (stats_ref[1:2, at] * fade + jnp.sum(p, axis=0, keepdims=True))
            fin_ref[0:1, at] = fade * inverse
            p = (p * inverse).astype(BF16)
            p_ref[head, :, here] = p
            return dot_nn(p, pair_rows(g_ref, pair))

        dv = added(per_head, unroll, step, total_ref).astype(BF16)
        for shift in range(shifts):
            back_ref[shift, :, cols] = dv[shift * own_keys : (shift + 1) * own_keys]


def far_value_kernel(
    unroll, q_ref, g_ref, v_ref, p_ref, fin_ref, near_v_ref, near_p_ref, *refs
):
    d_ref, stats_ref, back_ref, ds_ref, delta_ref, *total_ref = refs[2:]
    heads = v_ref.shape[1] // WIDTH
    per_head = q_ref.shape[1] // PAIR // heads
    shifts, own_keys, _ = back_ref.shape

    @pl.when(value_part_late())
    def value_part():
        near_value_work(g_ref, near_v_ref, near_p_ref, d_ref, stats_ref)

    for head in range(heads):
        cols = slice(head * WIDTH, (head + 1) * WIDTH)

        def step(i):
            pair = head * per_head + i
            at = columns(pair, PAIR)
            here = columns(i, PAIR)
            d = dot_nt(v_ref[:, cols], pair_rows(g_ref, pair))
            p = p_ref[head, :, here].astype(F32)
            delta = stats_ref[2:3, at] * fin_ref[0:1, at] + jnp.sum(p * d, axis=0, keepdims=True)
            delta_ref[0:1, at] = delta
            ds = (p * (d - delta)).astype(BF16)
            ds_ref[head, :, here] = ds
            return dot_nn(ds, pair_rows(q_ref, pair))

        dk = (added(per_head, unroll, step, total_ref) * SCALE).astype(BF16)
        for shift in range(shifts):
            back_ref[shift, :, cols] = dk[shift * own_keys : (shift + 1) * own_keys]


def sum_kernel(after_ref, own_ref, *refs):
    total = own_ref[...]
    for ref in refs[:-1]:
        total = total + ref[...].astype(F32)
    refs[-1][...] = total


def last_kernel(
    unroll, q_ref, g_ref, k_ref, p_ref, d_ref, fin_ref, delta_ref, fk_ref, fds_ref,
    dq_ref, dtk_ref, dtv_ref, dok_ref, dov_ref, low_ref, ds_ref,
):
    tail = dtk_ref.shape[0]
    heads = k_ref.shape[1] // WIDTH
    per_head = q_ref.shape[1] // PAIR // heads
    for head in range(heads):
        cols = slice(head * WIDTH, (head + 1) * WIDTH)

        def step(i):
            pair = head * per_head + i
            at = columns(pair, PAIR)
            here = columns(i, PAIR)
            p = p_ref[head, :, here] * fin_ref[0:1, at]
            ds = (p * (d_ref[head, :, here] - delta_ref[0:1, at])).astype(BF16)
            low_ref[head, :, here] = p.astype(BF16)
            ds_ref[head, :, here] = ds
            dq = dot_tn(k_ref[:, cols], ds) + dot_tn(fk_ref[:, cols], fds_ref[head, :, here])
            dq = dq * SCALE
            dq = jnp.concatenate([dq[:, :WIDTH].T, dq[:, WIDTH:].T], axis=1)
            dq_ref[:, at] = dq.astype(BF16)

        repeat(per_head, unroll, step)
        dk = dot_nn(ds_ref[head], stacked_rows(q_ref, head, 2 * per_head)) * SCALE
        dv = dot_nn(low_ref[head], stacked_rows(g_ref, head, 2 * per_head))
        dtk_ref[:, cols] = dk[:tail].astype(BF16)
        dtv_ref[:, cols] = dv[:tail].astype(BF16)
        dok_ref[:, cols] = dk[tail:]
        dov_ref[:, cols] = dv[tail:]


def call(kernel, spaces, outs, scratch, flops, mib, *args, aliases={}):
    vmem = pl.BlockSpec(memory_space=pltpu.VMEM)
    moved = sum(a.size * a.dtype.itemsize for a in args) + sum(
        math.prod(o.shape) * jnp.dtype(o.dtype).itemsize for o in outs
    )
    return pl.pallas_call(
        kernel,
        out_shape=outs,
        in_specs=[pl.BlockSpec(memory_space=space) for space in spaces],
        out_specs=[vmem] * len(outs),
        scratch_shapes=scratch,
        input_output_aliases=aliases,
        compiler_params=pltpu.CompilerParams(vmem_limit_bytes=mib * 2**20),
        cost_estimate=pl.CostEstimate(flops=flops, bytes_accessed=moved, transcendentals=0),
    )(*args)


def body(q, g, tk, tv, ck, cv, row_list, read_owner, read_tile, read_list, read_count):
    ctx = lax.axis_size("ctx")
    rows, q_width = q.shape
    kv_width = tk.shape[1]
    heads = kv_width // WIDTH
    group_rows = rows * (q_width // kv_width)
    own_keys = ck.shape[0]
    own = own_keys // TILE
    far_keys = (ctx - 1) * own_keys
    near_keys = rows + own_keys
    slots = -(-ctx * own // 8) * 8
    unroll = ctx <= 2
    row_list = row_list.reshape(1, rows)

    def shifted(x, shift):
        return lax.ppermute(x, "ctx", [(o, (o - shift) % ctx) for o in range(ctx)])

    far_k = [shifted(ck, s) for s in range(1, ctx)]
    shape = jax.ShapeDtypeStruct
    product = 2 * q_width * rows * WIDTH
    small = read_owner.shape
    here = [
        pltpu.with_memory_space_constraint(a, pltpu.HBM)
        for a in (q, g, tk, tv, ck, cv, row_list, read_owner, read_tile, read_list)
    ]
    near_outs = [
        pltpu.VMEM(q.shape, BF16),
        pltpu.VMEM(g.shape, BF16),
        pltpu.VMEM((near_keys, kv_width), BF16),
        pltpu.VMEM((near_keys, kv_width), BF16),
        pltpu.VMEM(row_list.shape, jnp.int32),
        pltpu.VMEM(small, jnp.int32),
        pltpu.VMEM(small, jnp.int32),
        pltpu.VMEM(small, jnp.int32),
        pltpu.VMEM((heads, near_keys, group_rows), F32),
        pltpu.VMEM((heads, near_keys, group_rows), F32),
        pltpu.VMEM((8, heads * group_rows), F32),
        pltpu.VMEM((slots, rows), F32),
    ]
    sems = [pltpu.SemaphoreType.DMA((10,))]
    flops = product * near_keys // WIDTH
    hbm = [pltpu.HBM] * len(here)
    early = list(
        call(functools.partial(near_kernel, ctx, True), hbm, near_outs, sems, flops, 32, *here)
    )
    own_v, early[-1] = lax.optimization_barrier((cv, early[-1]))
    far_v = [shifted(own_v, s) for s in range(1, ctx)]
    early = [pltpu.with_memory_space_constraint(a, pltpu.VMEM) for a in early]
    q, g, near_k, near_v, _, _, _, _, near_p, near_d, stats, table = call(
        functools.partial(near_kernel, ctx, False),
        hbm + [pltpu.SMEM] + [pltpu.VMEM] * NEAR_OUTS,
        near_outs,
        sems,
        flops,
        32,
        *here, read_count, *early,
        aliases={len(here) + 1 + i: i for i in range(NEAR_OUTS)},
    )
    mib = 32 if unroll else 60
    total = [] if unroll else [pltpu.VMEM((far_keys, WIDTH), F32)]
    far_k = far_k[0] if ctx == 2 else jnp.concatenate(far_k, axis=0)
    back_v, far_p, fin = call(
        functools.partial(far_key_kernel, unroll),
        [pltpu.VMEM] * 5,
        [
            shape((ctx - 1, own_keys, kv_width), BF16),
            shape((heads, far_keys, group_rows), BF16),
            shape((8, heads * group_rows), F32),
        ],
        total,
        2 * product * far_keys // WIDTH,
        mib,
        q, g, far_k, stats, table,
    )
    returned_v = [shifted(back_v[s - 1], -s) for s in range(1, ctx)]
    far_v = far_v[0] if ctx == 2 else jnp.concatenate(far_v, axis=0)
    near_d, stats = (pltpu.with_memory_space_constraint(a, pltpu.VMEM) for a in (near_d, stats))
    near_d, stats, back_k, far_ds, delta = call(
        functools.partial(far_value_kernel, unroll),
        [pltpu.VMEM] * 9,
        [
            pltpu.VMEM(near_d.shape, F32),
            pltpu.VMEM(stats.shape, F32),
            shape((ctx - 1, own_keys, kv_width), BF16),
            shape((heads, far_keys, group_rows), BF16),
            shape((8, heads * group_rows), F32),
        ],
        total,
        2 * product * far_keys // WIDTH,
        mib,
        q, g, far_v, far_p, fin, near_v, near_p, near_d, stats,
        aliases={7: 0, 8: 1},
    )
    returned_k = [shifted(back_k[s - 1], -s) for s in range(1, ctx)]
    dq, dtk, dtv, dok, dov = call(
        functools.partial(last_kernel, unroll),
        [pltpu.VMEM] * 9,
        [
            shape(q.shape, BF16),
            shape(tk.shape, BF16),
            shape(tv.shape, BF16),
            shape(ck.shape, F32),
            shape(cv.shape, F32),
        ],
        [pltpu.VMEM((heads, near_keys, group_rows), BF16)] * 2,
        product * (3 * near_keys + far_keys) // WIDTH,
        mib,
        q, g, near_k, near_p, near_d, fin, delta, far_k, far_ds,
    )

    def summed(after, own_sum, returned):
        return call(
            sum_kernel,
            [pltpu.HBM] + [pltpu.VMEM] * (1 + len(returned)),
            [shape(own_sum.shape, F32)],
            [],
            0,
            mib,
            pltpu.with_memory_space_constraint(after, pltpu.HBM), own_sum, *returned,
        )[0]

    dov = summed(dq, dov, returned_v)
    dok = summed(dov, dok, returned_k)
    return dq, dtk, dtv, dok, dov


def solution(mesh):
    wide = P(("dp", "ctx"), "tp")
    lone = P(("dp", "ctx"))
    flat = P(("dp", "ctx"), None)
    return jax.shard_map(
        body,
        mesh=mesh,
        in_specs=(wide,) * 6 + (lone, flat, flat, flat, lone),
        out_specs=(wide,) * 5,
        check_vma=False,
    )
```

profile of v0, /device:TPU:0, one launch (start us, length us, event | category | flops | bytes accessed | tf_op | source)
XLA Modules:
  0.0 17.9 jit_solution(3773238532735288189)
XLA Ops:
  0.6 3.0 %collective-permute-start.1 = (bf16[256,256]{1,0:T(8,128)(2,1)}, bf16[256,256]{1,0:T(8,128)(2,1)S(1)}, u32[]{:S(2)}, u32[]{:S(2)}) collective-permute-start(bf16[256,256]{1,0:T(8,128)(2,1)} %refs_4_.3), channel_id=1, source_target_pairs={{0,16},{16,0},{1,17},{17,1},{2,18},{18,2},{3,19},{19,3},{4,20},{20... | collective-permute-start | bytes 393224 | tf_op jit(solution)/shard_map/ppermute | solution.py:376
  3.6 0.1 shard_map.146
  3.7 0.1 collective-permute-start
  4.5 3.3 %shard_map.147 = (bf16[128,2048]{1,0:T(8,128)(2,1)S(1)}, bf16[128,2048]{1,0:T(8,128)(2,1)S(1)}, bf16[384,256]{1,0:T(8,128)(2,1)S(1)}, bf16[384,256]{1,0:T(8,128)...) custom-call(bf16[128,2048]{1,0:T(8,128)(2,1)} %refs_0_.3, ...), custom_call_target="tpu_custom_call", output_to_operand_aliasing={{0}: (11, {}), {1}: (12, {}), {2}: (13, {}), {3}: (14, {}),... | custom-call | flops 201326592 | bytes 17049956 | tf_op jit(solution)/shard_map/pallas_call | solution.py:349
  7.8 0.0 collective-permute-done.1.k_ref.fk_ref
  7.8 1.2 %shard_map.148 = (bf16[1,256,256]{2,1,0:T(8,128)(2,1)S(1)}, bf16[2,256,1024]{2,1,0:T(8,128)(2,1)S(1)}, f32[8,2048]{1,0:T(8,128)S(1)}) custom-call(bf16[128,2048]{1,0:T(8,128)(2,1)S(1)} %get-tuple-element.52.q_ref, bf16[128,2048]{1,0:T(8,128)(2,1)S(1)} %get-tuple-element.53.g_ref, bf16[256,256]{1,0:T(8,128)(2,1)S(1)} %collective-permute-done.1.k_ref.fk_ref, ...), custom_call_target="tpu_custom_call" | custom-call | flops 268435456 | bytes 2494464 | tf_op jit(solution)/shard_map/pallas_call | solution.py:349
  9.0 1.5 %collective-permute-start.2 = (bf16[256,256]{1,0:T(8,128)(2,1)S(1)}, bf16[256,256]{1,0:T(8,128)(2,1)S(1)}, u32[]{:S(2)}, u32[]{:S(2)}) collective-permute-start(bf16[256,256]{1,0:T(8,128)(2,1)S(1)} %bitcast.3), channel_id=1, source_target_pairs={{0,16},{16,0},{1,17},{17,1},{2,18},{18,2},{3,19},{19,3},{4,20},{20... | collective-permute-start | bytes 393224 | tf_op jit(solution)/shard_map/ppermute | solution.py:376
  10.5 0.0 collective-permute-done.v_ref
  10.5 1.1 %shard_map.149 = (f32[2,384,1024]{2,1,0:T(8,128)S(1)}, f32[8,2048]{1,0:T(8,128)S(1)}, bf16[1,256,256]{2,1,0:T(8,128)(2,1)S(1)}, bf16[2,256,1024]{2,1,0:T(8,128)(2,1)S(1)}, f32[8,2048]{1,0:T(8,128)S(1)}) custom-call(bf16[128,2048]{1,0:T(8,128)(2,1)S(1)} %get-tuple-element.52.q_ref, ...), custom_call_target="tpu_custom_call", output_to_operand_aliasing={{0}: (7, {}), {1}: (8, {})} | custom-call | flops 268435456 | bytes 13303808 | tf_op jit(solution)/shard_map/pallas_call | solution.py:349
  11.6 2.1 %collective-permute-start.3 = (bf16[256,256]{1,0:T(8,128)(2,1)S(1)}, bf16[256,256]{1,0:T(8,128)(2,1)S(1)}, u32[]{:S(2)}, u32[]{:S(2)}) collective-permute-start(bf16[256,256]{1,0:T(8,128)(2,1)S(1)} %bitcast.4), channel_id=1, source_target_pairs={{0,16},{16,0},{1,17},{17,1},{2,18},{18,2},{3,19},{19,3},{4,20},{20... | collective-permute-start | bytes 393224 | tf_op jit(solution)/shard_map/ppermute | solution.py:376
  13.7 2.3 %shard_map.150 = (bf16[128,2048]{1,0:T(8,128)(2,1)}, bf16[128,256]{1,0:T(8,128)(2,1)}, bf16[128,256]{1,0:T(8,128)(2,1)}, f32[256,256]{1,0:T(8,128)S(1)}, f32[256,256]{1,0:T(8,128)S(1)}) custom-call(bf16[128,2048]{1,0:T(8,128)(2,1)S(1)} %get-tuple-element.52.q_ref, bf16[128,2048]{1,0:T(8,128)(2,1)S(1)} %get-tuple-element.53.g_ref, ...), custom_call_target="tpu_custom_call" | custom-call | flops 738197504 | bytes 10027008 | tf_op jit(solution)/shard_map/pallas_call | solution.py:349
  16.0 0.0 collective-permute-done.2.refs_0_
  16.0 0.7 %shard_map.151.after_ref = f32[256,256]{1,0:T(8,128)} custom-call(bf16[128,2048]{1,0:T(8,128)(2,1)} %get-tuple-element.34.after_ref, f32[256,256]{1,0:T(8,128)S(1)} %get-tuple-element.69.own_ref, bf16[256,256]{1,0:T(8,128)(2,1)S(1)} %collective-permute-done.2.refs_0_), custom_call_target="tpu_custom_call" | custom-call | bytes 1179648 | tf_op jit(solution)/shard_map/pallas_call | solution.py:349
  16.7 0.5 %collective-permute-done.3.refs_0_ = bf16[256,256]{1,0:T(8,128)(2,1)S(1)} collective-permute-done((bf16[256,256]{1,0:T(8,128)(2,1)S(1)}, bf16[256,256]{1,0:T(8,128)(2,1)S(1)}, u32[]{:S(2)}, u32[]{:S(2)}) %collective-permute-start.3) | collective-permute-done | bytes 131104 | tf_op jit(solution)/shard_map/ppermute | solution.py:376
  17.2 0.7 %shard_map.152 = f32[256,256]{1,0:T(8,128)} custom-call(f32[256,256]{1,0:T(8,128)} %shard_map.151.after_ref, f32[256,256]{1,0:T(8,128)S(1)} %get-tuple-element.71.own_ref, bf16[256,256]{1,0:T(8,128)(2,1)S(1)} %collective-permute-done.3.refs_0_), custom_call_target="tpu_custom_call" | custom-call | bytes 917504 | tf_op jit(solution)/shard_map/pallas_call | solution.py:349
Async XLA Ops:
  0.6 7.2 %collective-permute-start.1 = (bf16[256,256]{1,0:T(8,128)(2,1)}, bf16[256,256]{1,0:T(8,128)(2,1)S(1)}, u32[]{:S(2)}, u32[]{:S(2)}) collective-permute-start(bf16[256,256]{1,0:T(8,128)(2,1)} %refs_4_.3), channel_id=1, source_target_pairs={{0,16},{16,0},{1,17},{17,1},{2,18},{18,2},{3,19},{19,3},{4,20},{20... | collective-permute-start | bytes 393224 | tf_op jit(solution)/shard_map/ppermute | solution.py:376
  3.7 6.7 %collective-permute-start = (bf16[256,256]{1,0:T(8,128)(2,1)}, bf16[256,256]{1,0:T(8,128)(2,1)S(1)}, u32[]{:S(2)}, u32[]{:S(2)}) collective-permute-start(bf16[256,256]{1,0:T(8,128)(2,1)} %refs_5_.3), channel_id=1, source_target_pairs={{0,16},{16,0},{1,17},{17,1},{2,18},{18,2},{3,19},{19,3},{4,20},{20... | collective-permute-start | bytes 393224 | tf_op jit(solution)/shard_map/ppermute | solution.py:376
  9.0 7.0 %collective-permute-start.2 = (bf16[256,256]{1,0:T(8,128)(2,1)S(1)}, bf16[256,256]{1,0:T(8,128)(2,1)S(1)}, u32[]{:S(2)}, u32[]{:S(2)}) collective-permute-start(bf16[256,256]{1,0:T(8,128)(2,1)S(1)} %bitcast.3), channel_id=1, source_target_pairs={{0,16},{16,0},{1,17},{17,1},{2,18},{18,2},{3,19},{19,3},{4,20},{20... | collective-permute-start | bytes 393224 | tf_op jit(solution)/shard_map/ppermute | solution.py:376
  11.6 5.6 %collective-permute-start.3 = (bf16[256,256]{1,0:T(8,128)(2,1)S(1)}, bf16[256,256]{1,0:T(8,128)(2,1)S(1)}, u32[]{:S(2)}, u32[]{:S(2)}) collective-permute-start(bf16[256,256]{1,0:T(8,128)(2,1)S(1)} %bitcast.4), channel_id=1, source_target_pairs={{0,16},{16,0},{1,17},{17,1},{2,18},{18,2},{3,19},{19,3},{4,20},{20... | collective-permute-start | bytes 393224 | tf_op jit(solution)/shard_map/ppermute | solution.py:376
where the time goes:
time: 18.1 us; the launch traced here: 17.9 us
  Pallas kernels  9.45 us (52%)
  starting transfers between devices  6.66 us (37%)
  between operations  1.32 us (7%)
  waiting for transfers between devices  0.5 us (3%)
    pallas_call x7, Pallas kernels, call(): pl.pallas_call(kernel, out_shape=outs, in_specs=[pl.BlockSpec(memory_spac...  9.45 us
    ppermute x4, starting transfers between devices, shifted(): return lax.ppermute(x, 'ctx', [(o, (o - shift) % ctx) for o in range(ctx)])  6.66 us
    ppermute x4, waiting for transfers between devices, shifted(): return lax.ppermute(x, 'ctx', [(o, (o - shift) % ctx) for o in range(ctx)])  0.5 us
  transfers between devices with their start and end apart: 4, of which 1 were waited for; matrix products, arithmetic and copies ran while one was open for 0% of the time, Pallas kernels for 49%

commit v1 on v0

--- a/solution.py
+++ b/solution.py
@@ -134,9 +134,11 @@
 
 
 def near_key_work(
-    ctx, own, raw_made, q_ref, k_ref, p_ref, stats_ref, table_ref,
+    ctx, own, copies, q_ref, k_ref, p_ref, stats_ref, table_ref,
     rl_ref, ro_ref, rt_ref, rs_ref, rc_ref,
 ):
+    for copy in copies[:4]:
+        copy.wait()
     heads = k_ref.shape[1] // WIDTH
     per_head = q_ref.shape[1] // PAIR // heads
     reads = ro_ref.shape[1]
@@ -155,20 +157,24 @@
     table = jnp.where(count > 0.5, jnp.log2(jnp.maximum(count, 1.0)), NEG)
     table_ref[...] = table
     biases = [tail_bias(row_list)] + tile_bias(table, 0, own)
+    for copy in copies[4:7]:
+        copy.wait()
     for head in range(heads):
         for i in range(per_head):
             at = columns(head * per_head + i, PAIR)
             here = columns(i, PAIR)
-            if raw_made:
+            if copies:
+                raw = raw_scores(q_ref, k_ref, head, i, per_head)
+            else:
                 raw = p_ref[head, :, here]
-            else:
-                raw = raw_scores(q_ref, k_ref, head, i, per_head)
             s = add_tiles(raw, biases)
             top = jnp.max(s, axis=0, keepdims=True)
             p = jnp.exp2(s - top)
             p_ref[head, :, here] = p
             stats_ref[0:1, at] = top
             stats_ref[1:2, at] = jnp.sum(p, axis=0, keepdims=True)
+    for copy in copies[7:]:
+        copy.wait()
 
 
 def near_dprob_work(g_ref, v_ref, d_ref):
@@ -208,15 +214,14 @@
     p_ref, d_ref, stats_ref, table_ref, sems = rest[8:]
 
     def load():
-        copies = load_copies(ins, q_ref, g_ref, k_ref, v_ref, small_refs, sems)
-        for copy in copies:
-            copy.wait()
+        return load_copies(ins, q_ref, g_ref, k_ref, v_ref, small_refs, sems)
 
     if early:
 
         @pl.when(is_odd())
         def first_part():
-            load()
+            for copy in load():
+                copy.wait()
             near_raw_work(q_ref, k_ref, p_ref)
             near_dprob_work(g_ref, v_ref, d_ref)
 
@@ -226,13 +231,12 @@
 
     @pl.when(is_odd())
     def rest_of_it():
-        near_key_work(ctx, own, True, *refs_of_keys)
+        near_key_work(ctx, own, [], *refs_of_keys)
         near_cross_work(p_ref, d_ref, stats_ref)
 
     @pl.when(jnp.logical_not(is_odd()))
     def key_part():
-        load()
-        near_key_work(ctx, own, False, *refs_of_keys)
+        near_key_work(ctx, own, load(), *refs_of_keys)
 
     @pl.when(jnp.logical_not(jnp.logical_or(is_odd(), value_part_late())))
     def value_part():
@@ -270,17 +274,18 @@
             back_ref[shift, :, cols] = dv[shift * own_keys : (shift + 1) * own_keys]
 
 
+def late_near_kernel(after_ref, g_ref, v_ref, p_ref, d_in, stats_in, d_ref, stats_ref):
+    @pl.when(value_part_late())
+    def value_part():
+        near_value_work(g_ref, v_ref, p_ref, d_ref, stats_ref)
+
+
 def far_value_kernel(
-    unroll, q_ref, g_ref, v_ref, p_ref, fin_ref, near_v_ref, near_p_ref, *refs
+    unroll, q_ref, g_ref, v_ref, p_ref, fin_ref, stats_ref, back_ref, ds_ref, delta_ref, *total_ref
 ):
-    d_ref, stats_ref, back_ref, ds_ref, delta_ref, *total_ref = refs[2:]
     heads = v_ref.shape[1] // WIDTH
     per_head = q_ref.shape[1] // PAIR // heads
     shifts, own_keys, _ = back_ref.shape
-
-    @pl.when(value_part_late())
-    def value_part():
-        near_value_work(g_ref, near_v_ref, near_p_ref, d_ref, stats_ref)
 
     for head in range(heads):
         cols = slice(head * WIDTH, (head + 1) * WIDTH)
@@ -435,12 +440,20 @@
     returned_v = [shifted(back_v[s - 1], -s) for s in range(1, ctx)]
     far_v = far_v[0] if ctx == 2 else jnp.concatenate(far_v, axis=0)
     near_d, stats = (pltpu.with_memory_space_constraint(a, pltpu.VMEM) for a in (near_d, stats))
-    near_d, stats, back_k, far_ds, delta = call(
+    near_d, stats = call(
+        late_near_kernel,
+        [pltpu.VMEM] * 6,
+        [pltpu.VMEM(near_d.shape, F32), pltpu.VMEM(stats.shape, F32)],
+        [],
+        flops,
+        32,
+        fin, g, near_v, near_p, near_d, stats,
+        aliases={4: 0, 5: 1},
+    )
+    back_k, far_ds, delta = call(
         functools.partial(far_value_kernel, unroll),
-        [pltpu.VMEM] * 9,
+        [pltpu.VMEM] * 6,
         [
-            pltpu.VMEM(near_d.shape, F32),
-            pltpu.VMEM(stats.shape, F32),
             shape((ctx - 1, own_keys, kv_width), BF16),
             shape((heads, far_keys, group_rows), BF16),
             shape((8, heads * group_rows), F32),
@@ -448,8 +461,7 @@
         total,
         2 * product * far_keys // WIDTH,
         mib,
-        q, g, far_v, far_p, fin, near_v, near_p, near_d, stats,
-        aliases={7: 0, 8: 1},
+        q, g, far_v, far_p, fin, stats,
     )
     returned_k = [shifted(back_k[s - 1], -s) for s in range(1, ctx)]
     dq, dtk, dtv, dok, dov = call(

time: 18.1 us -> 18.1 us (level)
  waiting for transfers between devices: 0.5 us -> 1.09 us
  starting transfers between devices: 6.66 us -> 6.29 us
  Pallas kernels: 9.45 us -> 9.22 us
    ppermute x4, waiting for transfers between devices: 0.5 us -> 1.09 us  [shifted(): return lax.ppermute(x, 'ctx', [(o, (o - shift) % ctx) for o in range(ctx)])]
    ppermute x4, starting transfers between devices: 6.66 us -> 6.29 us  [shifted(): return lax.ppermute(x, 'ctx', [(o, (o - shift) % ctx) for o in range(ctx)])]
    pallas_call x7 -> x8, Pallas kernels: 9.45 us -> 9.22 us  [call(): pl.pallas_call(kernel, out_shape=outs, in_specs=[pl.BlockSpec(memory_spac...]
  transfers between devices with their start and end apart: 4 -> 4, of which waited for: 1 -> 1; matrix products, arithmetic and copies ran while one was open for 0% -> 0% of each run, Pallas kernels for 49% -> 47%
where the time goes in v1:
time: 18.1 us; the launch traced here: 17.9 us
  Pallas kernels  9.22 us (51%)
  starting transfers between devices  6.29 us (35%)
  between operations  1.32 us (7%)
  waiting for transfers between devices  1.09 us (6%)
    pallas_call x8, Pallas kernels, call(): pl.pallas_call(kernel, out_shape=outs, in_specs=[pl.BlockSpec(memory_spac...  9.22 us
    ppermute x4, starting transfers between devices, shifted(): return lax.ppermute(x, 'ctx', [(o, (o - shift) % ctx) for o in range(ctx)])  6.29 us
    ppermute x4, waiting for transfers between devices, shifted(): return lax.ppermute(x, 'ctx', [(o, (o - shift) % ctx) for o in range(ctx)])  1.09 us
  transfers between devices with their start and end apart: 4, of which 1 were waited for; matrix products, arithmetic and copies ran while one was open for 0% of the time, Pallas kernels for 47%

profile of v1, /device:TPU:0, one launch (start us, length us, event | category | flops | bytes accessed | tf_op | source)
XLA Modules:
  0.0 17.9 jit_solution(2370220101454509418)
XLA Ops:
  0.6 3.0 %collective-permute-start = (bf16[256,256]{1,0:T(8,128)(2,1)}, bf16[256,256]{1,0:T(8,128)(2,1)S(1)}, u32[]{:S(2)}, u32[]{:S(2)}) collective-permute-start(bf16[256,256]{1,0:T(8,128)(2,1)} %refs_4_.3), channel_id=1, source_target_pairs={{0,16},{16,0},{1,17},{17,1},{2,18},{18,2},{3,19},{19,3},{4,20},{20... | collective-permute-start | bytes 393224 | tf_op jit(solution)/shard_map/ppermute | solution.py:381
  3.6 0.1 shard_map.146
  3.7 0.1 collective-permute-start.1
  4.5 3.1 %shard_map.147 = (bf16[128,2048]{1,0:T(8,128)(2,1)S(1)}, bf16[128,2048]{1,0:T(8,128)(2,1)S(1)}, bf16[384,256]{1,0:T(8,128)(2,1)S(1)}, bf16[384,256]{1,0:T(8,128)...) custom-call(bf16[128,2048]{1,0:T(8,128)(2,1)} %refs_0_.3, ...), custom_call_target="tpu_custom_call", output_to_operand_aliasing={{0}: (11, {}), {1}: (12, {}), {2}: (13, {}), {3}: (14, {}),... | custom-call | flops 201326592 | bytes 17049956 | tf_op jit(solution)/shard_map/pallas_call | solution.py:354
  7.6 0.0 collective-permute-done.k_ref.fk_ref
  7.6 1.2 %shard_map.148 = (bf16[1,256,256]{2,1,0:T(8,128)(2,1)S(1)}, bf16[2,256,1024]{2,1,0:T(8,128)(2,1)S(1)}, f32[8,2048]{1,0:T(8,128)S(1)}) custom-call(bf16[128,2048]{1,0:T(8,128)(2,1)S(1)} %get-tuple-element.53.q_ref, bf16[128,2048]{1,0:T(8,128)(2,1)S(1)} %get-tuple-element.54.g_ref, bf16[256,256]{1,0:T(8,128)(2,1)S(1)} %collective-permute-done.k_ref.fk_ref, ...), custom_call_target="tpu_custom_call" | custom-call | flops 268435456 | bytes 2494464 | tf_op jit(solution)/shard_map/pallas_call | solution.py:354
  8.8 1.7 %collective-permute-start.2 = (bf16[256,256]{1,0:T(8,128)(2,1)S(1)}, bf16[256,256]{1,0:T(8,128)(2,1)S(1)}, u32[]{:S(2)}, u32[]{:S(2)}) collective-permute-start(bf16[256,256]{1,0:T(8,128)(2,1)S(1)} %bitcast.3), channel_id=1, source_target_pairs={{0,16},{16,0},{1,17},{17,1},{2,18},{18,2},{3,19},{19,3},{4,20},{20... | collective-permute-start | bytes 393224 | tf_op jit(solution)/shard_map/ppermute | solution.py:381
  10.5 0.0 collective-permute-done.1.v_ref
  10.5 1.1 %shard_map.150 = (bf16[1,256,256]{2,1,0:T(8,128)(2,1)S(1)}, bf16[2,256,1024]{2,1,0:T(8,128)(2,1)S(1)}, f32[8,2048]{1,0:T(8,128)S(1)}) custom-call(bf16[128,2048]{1,0:T(8,128)(2,1)S(1)} %get-tuple-element.53.q_ref, bf16[128,2048]{1,0:T(8,128)(2,1)S(1)} %get-tuple-element.54.g_ref, bf16[256,256]{1,0:T(8,128)(2,1)S(1)} %collective-permute-done.1.v_ref, ...), custom_call_target="tpu_custom_call" | custom-call | flops 268435456 | bytes 3604480 | tf_op jit(solution)/shard_map/pallas_call | solution.py:354
  11.6 1.5 %collective-permute-start.3 = (bf16[256,256]{1,0:T(8,128)(2,1)S(1)}, bf16[256,256]{1,0:T(8,128)(2,1)S(1)}, u32[]{:S(2)}, u32[]{:S(2)}) collective-permute-start(bf16[256,256]{1,0:T(8,128)(2,1)S(1)} %bitcast.4), channel_id=1, source_target_pairs={{0,16},{16,0},{1,17},{17,1},{2,18},{18,2},{3,19},{19,3},{4,20},{20... | collective-permute-start | bytes 393224 | tf_op jit(solution)/shard_map/ppermute | solution.py:381
  13.1 2.3 %shard_map.151 = (bf16[128,2048]{1,0:T(8,128)(2,1)}, bf16[128,256]{1,0:T(8,128)(2,1)}, bf16[128,256]{1,0:T(8,128)(2,1)}, f32[256,256]{1,0:T(8,128)S(1)}, f32[256,256]{1,0:T(8,128)S(1)}) custom-call(bf16[128,2048]{1,0:T(8,128)(2,1)S(1)} %get-tuple-element.53.q_ref, bf16[128,2048]{1,0:T(8,128)(2,1)S(1)} %get-tuple-element.54.g_ref, ...), custom_call_target="tpu_custom_call" | custom-call | flops 738197504 | bytes 10027008 | tf_op jit(solution)/shard_map/pallas_call | solution.py:354
  15.4 0.0 collective-permute-done.2.refs_0_
  15.4 0.7 %shard_map.152.after_ref = f32[256,256]{1,0:T(8,128)} custom-call(bf16[128,2048]{1,0:T(8,128)(2,1)} %get-tuple-element.35.after_ref, f32[256,256]{1,0:T(8,128)S(1)} %get-tuple-element.71.own_ref, bf16[256,256]{1,0:T(8,128)(2,1)S(1)} %collective-permute-done.2.refs_0_), custom_call_target="tpu_custom_call" | custom-call | bytes 1179648 | tf_op jit(solution)/shard_map/pallas_call | solution.py:354
  16.1 1.1 %collective-permute-done.3.refs_0_ = bf16[256,256]{1,0:T(8,128)(2,1)S(1)} collective-permute-done((bf16[256,256]{1,0:T(8,128)(2,1)S(1)}, bf16[256,256]{1,0:T(8,128)(2,1)S(1)}, u32[]{:S(2)}, u32[]{:S(2)}) %collective-permute-start.3) | collective-permute-done | bytes 131104 | tf_op jit(solution)/shard_map/ppermute | solution.py:381
  17.2 0.7 %shard_map.153 = f32[256,256]{1,0:T(8,128)} custom-call(f32[256,256]{1,0:T(8,128)} %shard_map.152.after_ref, f32[256,256]{1,0:T(8,128)S(1)} %get-tuple-element.73.own_ref, bf16[256,256]{1,0:T(8,128)(2,1)S(1)} %collective-permute-done.3.refs_0_), custom_call_target="tpu_custom_call" | custom-call | bytes 917504 | tf_op jit(solution)/shard_map/pallas_call | solution.py:354
  (1 shorter events, 0.0 us)
Async XLA Ops:
  0.6 7.0 %collective-permute-start = (bf16[256,256]{1,0:T(8,128)(2,1)}, bf16[256,256]{1,0:T(8,128)(2,1)S(1)}, u32[]{:S(2)}, u32[]{:S(2)}) collective-permute-start(bf16[256,256]{1,0:T(8,128)(2,1)} %refs_4_.3), channel_id=1, source_target_pairs={{0,16},{16,0},{1,17},{17,1},{2,18},{18,2},{3,19},{19,3},{4,20},{20... | collective-permute-start | bytes 393224 | tf_op jit(solution)/shard_map/ppermute | solution.py:381
  3.7 6.7 %collective-permute-start.1 = (bf16[256,256]{1,0:T(8,128)(2,1)}, bf16[256,256]{1,0:T(8,128)(2,1)S(1)}, u32[]{:S(2)}, u32[]{:S(2)}) collective-permute-start(bf16[256,256]{1,0:T(8,128)(2,1)} %refs_5_.3), channel_id=1, source_target_pairs={{0,16},{16,0},{1,17},{17,1},{2,18},{18,2},{3,19},{19,3},{4,20},{20... | collective-permute-start | bytes 393224 | tf_op jit(solution)/shard_map/ppermute | solution.py:381
  8.8 6.6 %collective-permute-start.2 = (bf16[256,256]{1,0:T(8,128)(2,1)S(1)}, bf16[256,256]{1,0:T(8,128)(2,1)S(1)}, u32[]{:S(2)}, u32[]{:S(2)}) collective-permute-start(bf16[256,256]{1,0:T(8,128)(2,1)S(1)} %bitcast.3), channel_id=1, source_target_pairs={{0,16},{16,0},{1,17},{17,1},{2,18},{18,2},{3,19},{19,3},{4,20},{20... | collective-permute-start | bytes 393224 | tf_op jit(solution)/shard_map/ppermute | solution.py:381
  11.6 5.6 %collective-permute-start.3 = (bf16[256,256]{1,0:T(8,128)(2,1)S(1)}, bf16[256,256]{1,0:T(8,128)(2,1)S(1)}, u32[]{:S(2)}, u32[]{:S(2)}) collective-permute-start(bf16[256,256]{1,0:T(8,128)(2,1)S(1)} %bitcast.4), channel_id=1, source_target_pairs={{0,16},{16,0},{1,17},{17,1},{2,18},{18,2},{3,19},{19,3},{4,20},{20... | collective-permute-start | bytes 393224 | tf_op jit(solution)/shard_map/ppermute | solution.py:381

commit v2 on v1

--- a/solution.py
+++ b/solution.py
@@ -107,14 +107,14 @@
     return jnp.logical_and(jnp.logical_not(is_odd()), lax.axis_index("ctx") > 0)
 
 
-def load_copies(ins, q_ref, g_ref, k_ref, v_ref, small_refs, sems):
+def load_copies(which, ins, q_ref, g_ref, k_ref, v_ref, small_refs, sems):
     q_in, g_in, tk_in, tv_in, ok_in, ov_in, *small_ins = ins
     tail = tk_in.shape[0]
     moves = list(zip(small_ins, small_refs)) + [
         (tk_in, k_ref.at[:tail]), (ok_in, k_ref.at[tail:]), (q_in, q_ref),
         (tv_in, v_ref.at[:tail]), (ov_in, v_ref.at[tail:]), (g_in, g_ref),
     ]
-    copies = [pltpu.make_async_copy(a, b, sems.at[i]) for i, (a, b) in enumerate(moves)]
+    copies = [pltpu.make_async_copy(*moves[i], sems.at[i]) for i in which]
     for copy in copies:
         copy.start()
     return copies
@@ -157,8 +157,6 @@
     table = jnp.where(count > 0.5, jnp.log2(jnp.maximum(count, 1.0)), NEG)
     table_ref[...] = table
     biases = [tail_bias(row_list)] + tile_bias(table, 0, own)
-    for copy in copies[4:7]:
-        copy.wait()
     for head in range(heads):
         for i in range(per_head):
             at = columns(head * per_head + i, PAIR)
@@ -173,7 +171,7 @@
             p_ref[head, :, here] = p
             stats_ref[0:1, at] = top
             stats_ref[1:2, at] = jnp.sum(p, axis=0, keepdims=True)
-    for copy in copies[7:]:
+    for copy in copies[4:]:
         copy.wait()
 
 
@@ -213,17 +211,22 @@
     q_ref, g_ref, k_ref, v_ref, *small_refs = rest[:8]
     p_ref, d_ref, stats_ref, table_ref, sems = rest[8:]
 
-    def load():
-        return load_copies(ins, q_ref, g_ref, k_ref, v_ref, small_refs, sems)
+    def load(which):
+        return load_copies(which, ins, q_ref, g_ref, k_ref, v_ref, small_refs, sems)
 
     if early:
 
         @pl.when(is_odd())
         def first_part():
-            for copy in load():
+            for copy in load(range(10)):
                 copy.wait()
             near_raw_work(q_ref, k_ref, p_ref)
             near_dprob_work(g_ref, v_ref, d_ref)
+
+        @pl.when(jnp.logical_not(is_odd()))
+        def keys_only():
+            for copy in load((4, 5, 6)):
+                copy.wait()
 
         return
     own = ins[4].shape[0] // TILE
@@ -236,7 +239,7 @@
 
     @pl.when(jnp.logical_not(is_odd()))
     def key_part():
-        near_key_work(ctx, own, load(), *refs_of_keys)
+        near_key_work(ctx, own, load((0, 1, 2, 3, 7, 8, 9)), *refs_of_keys)
 
     @pl.when(jnp.logical_not(jnp.logical_or(is_odd(), value_part_late())))
     def value_part():

time: 18.1 us -> 18.8 us (1.039)
  waiting for transfers between devices: 1.09 us -> 2.05 us
  starting transfers between devices: 6.29 us -> 5.41 us
  Pallas kernels: 9.22 us -> 9.87 us
    ppermute x4, waiting for transfers between devices: 1.09 us -> 2.05 us  [shifted(): return lax.ppermute(x, 'ctx', [(o, (o - shift) % ctx) for o in range(ctx)])]
    ppermute x4, starting transfers between devices: 6.29 us -> 5.41 us  [shifted(): return lax.ppermute(x, 'ctx', [(o, (o - shift) % ctx) for o in range(ctx)])]
    pallas_call x8, Pallas kernels: 9.22 us -> 9.87 us  [call(): pl.pallas_call(kernel, out_shape=outs, in_specs=[pl.BlockSpec(memory_spac...]
  transfers between devices with their start and end apart: 4 -> 4, of which waited for: 1 -> 2; matrix products, arithmetic and copies ran while one was open for 0% -> 0% of each run, Pallas kernels for 47% -> 49%
where the time goes in v2:
time: 18.8 us; the launch traced here: 18.7 us
  Pallas kernels  9.87 us (52%)
  starting transfers between devices  5.41 us (29%)
  waiting for transfers between devices  2.05 us (11%)
  between operations  1.32 us (7%)
    pallas_call x8, Pallas kernels, call(): pl.pallas_call(kernel, out_shape=outs, in_specs=[pl.BlockSpec(memory_spac...  9.87 us
    ppermute x4, starting transfers between devices, shifted(): return lax.ppermute(x, 'ctx', [(o, (o - shift) % ctx) for o in range(ctx)])  5.41 us
    ppermute x4, waiting for transfers between devices, shifted(): return lax.ppermute(x, 'ctx', [(o, (o - shift) % ctx) for o in range(ctx)])  2.05 us
  transfers between devices with their start and end apart: 4, of which 2 were waited for; matrix products, arithmetic and copies ran while one was open for 0% of the time, Pallas kernels for 49%

profile of v2, /device:TPU:0, one launch (start us, length us, event | category | flops | bytes accessed | tf_op | source)
XLA Modules:
  0.0 18.7 jit_solution(11144290657574194730)
XLA Ops:
  0.6 3.0 %collective-permute-start = (bf16[256,256]{1,0:T(8,128)(2,1)}, bf16[256,256]{1,0:T(8,128)(2,1)S(1)}, u32[]{:S(2)}, u32[]{:S(2)}) collective-permute-start(bf16[256,256]{1,0:T(8,128)(2,1)} %refs_4_.3), channel_id=1, source_target_pairs={{0,16},{16,0},{1,17},{17,1},{2,18},{18,2},{3,19},{19,3},{4,20},{20... | collective-permute-start | bytes 393224 | tf_op jit(solution)/shard_map/ppermute | solution.py:384
  3.6 1.2 %shard_map.146 = (bf16[128,2048]{1,0:T(8,128)(2,1)S(1)}, bf16[128,2048]{1,0:T(8,128)(2,1)S(1)}, bf16[384,256]{1,0:T(8,128)(2,1)S(1)}, bf16[384,256]{1,0:T(8,128)...) custom-call(bf16[128,2048]{1,0:T(8,128)(2,1)} %refs_0_.3, ...), custom_call_target="tpu_custom_call" | custom-call | flops 201326592 | bytes 9246272 | tf_op jit(solution)/shard_map/pallas_call | solution.py:357
  4.9 0.1 collective-permute-start.1
  5.6 2.6 %shard_map.147 = (bf16[128,2048]{1,0:T(8,128)(2,1)S(1)}, bf16[128,2048]{1,0:T(8,128)(2,1)S(1)}, bf16[384,256]{1,0:T(8,128)(2,1)S(1)}, bf16[384,256]{1,0:T(8,128)...) custom-call(bf16[128,2048]{1,0:T(8,128)(2,1)} %refs_0_.3, ...), custom_call_target="tpu_custom_call", output_to_operand_aliasing={{0}: (11, {}), {1}: (12, {}), {2}: (13, {}), {3}: (14, {}),... | custom-call | flops 201326592 | bytes 17049956 | tf_op jit(solution)/shard_map/pallas_call | solution.py:357
  8.3 0.0 collective-permute-done.k_ref.fk_ref
  8.3 1.2 %shard_map.148 = (bf16[1,256,256]{2,1,0:T(8,128)(2,1)S(1)}, bf16[2,256,1024]{2,1,0:T(8,128)(2,1)S(1)}, f32[8,2048]{1,0:T(8,128)S(1)}) custom-call(bf16[128,2048]{1,0:T(8,128)(2,1)S(1)} %get-tuple-element.53.q_ref, bf16[128,2048]{1,0:T(8,128)(2,1)S(1)} %get-tuple-element.54.g_ref, bf16[256,256]{1,0:T(8,128)(2,1)S(1)} %collective-permute-done.k_ref.fk_ref, ...), custom_call_target="tpu_custom_call" | custom-call | flops 268435456 | bytes 2494464 | tf_op jit(solution)/shard_map/pallas_call | solution.py:357
  9.4 1.5 %collective-permute-start.2 = (bf16[256,256]{1,0:T(8,128)(2,1)S(1)}, bf16[256,256]{1,0:T(8,128)(2,1)S(1)}, u32[]{:S(2)}, u32[]{:S(2)}) collective-permute-start(bf16[256,256]{1,0:T(8,128)(2,1)S(1)} %bitcast.3), channel_id=1, source_target_pairs={{0,16},{16,0},{1,17},{17,1},{2,18},{18,2},{3,19},{19,3},{4,20},{20... | collective-permute-start | bytes 393224 | tf_op jit(solution)/shard_map/ppermute | solution.py:384
  10.9 0.5 %collective-permute-done.1.v_ref = bf16[256,256]{1,0:T(8,128)(2,1)S(1)} collective-permute-done((bf16[256,256]{1,0:T(8,128)(2,1)}, bf16[256,256]{1,0:T(8,128)(2,1)S(1)}, u32[]{:S(2)}, u32[]{:S(2)}) %collective-permute-start.1) | collective-permute-done | bytes 131104 | tf_op jit(solution)/shard_map/ppermute | solution.py:384
  11.4 1.1 %shard_map.150 = (bf16[1,256,256]{2,1,0:T(8,128)(2,1)S(1)}, bf16[2,256,1024]{2,1,0:T(8,128)(2,1)S(1)}, f32[8,2048]{1,0:T(8,128)S(1)}) custom-call(bf16[128,2048]{1,0:T(8,128)(2,1)S(1)} %get-tuple-element.53.q_ref, bf16[128,2048]{1,0:T(8,128)(2,1)S(1)} %get-tuple-element.54.g_ref, bf16[256,256]{1,0:T(8,128)(2,1)S(1)} %collective-permute-done.1.v_ref, ...), custom_call_target="tpu_custom_call" | custom-call | flops 268435456 | bytes 3604480 | tf_op jit(solution)/shard_map/pallas_call | solution.py:357
  12.5 0.8 %collective-permute-start.3 = (bf16[256,256]{1,0:T(8,128)(2,1)S(1)}, bf16[256,256]{1,0:T(8,128)(2,1)S(1)}, u32[]{:S(2)}, u32[]{:S(2)}) collective-permute-start(bf16[256,256]{1,0:T(8,128)(2,1)S(1)} %bitcast.4), channel_id=1, source_target_pairs={{0,16},{16,0},{1,17},{17,1},{2,18},{18,2},{3,19},{19,3},{4,20},{20... | collective-permute-start | bytes 393224 | tf_op jit(solution)/shard_map/ppermute | solution.py:384
  13.3 2.3 %shard_map.151 = (bf16[128,2048]{1,0:T(8,128)(2,1)}, bf16[128,256]{1,0:T(8,128)(2,1)}, bf16[128,256]{1,0:T(8,128)(2,1)}, f32[256,256]{1,0:T(8,128)S(1)}, f32[256,256]{1,0:T(8,128)S(1)}) custom-call(bf16[128,2048]{1,0:T(8,128)(2,1)S(1)} %get-tuple-element.53.q_ref, bf16[128,2048]{1,0:T(8,128)(2,1)S(1)} %get-tuple-element.54.g_ref, ...), custom_call_target="tpu_custom_call" | custom-call | flops 738197504 | bytes 10027008 | tf_op jit(solution)/shard_map/pallas_call | solution.py:357
  15.6 0.0 collective-permute-done.2.refs_0_
  15.6 0.7 %shard_map.152.after_ref = f32[256,256]{1,0:T(8,128)} custom-call(bf16[128,2048]{1,0:T(8,128)(2,1)} %get-tuple-element.35.after_ref, f32[256,256]{1,0:T(8,128)S(1)} %get-tuple-element.71.own_ref, bf16[256,256]{1,0:T(8,128)(2,1)S(1)} %collective-permute-done.2.refs_0_), custom_call_target="tpu_custom_call" | custom-call | bytes 1179648 | tf_op jit(solution)/shard_map/pallas_call | solution.py:357
  16.4 1.6 %collective-permute-done.3.refs_0_ = bf16[256,256]{1,0:T(8,128)(2,1)S(1)} collective-permute-done((bf16[256,256]{1,0:T(8,128)(2,1)S(1)}, bf16[256,256]{1,0:T(8,128)(2,1)S(1)}, u32[]{:S(2)}, u32[]{:S(2)}) %collective-permute-start.3) | collective-permute-done | bytes 131104 | tf_op jit(solution)/shard_map/ppermute | solution.py:384
  17.9 0.7 %shard_map.153 = f32[256,256]{1,0:T(8,128)} custom-call(f32[256,256]{1,0:T(8,128)} %shard_map.152.after_ref, f32[256,256]{1,0:T(8,128)S(1)} %get-tuple-element.73.own_ref, bf16[256,256]{1,0:T(8,128)(2,1)S(1)} %collective-permute-done.3.refs_0_), custom_call_target="tpu_custom_call" | custom-call | bytes 917504 | tf_op jit(solution)/shard_map/pallas_call | solution.py:357
  (1 shorter events, 0.0 us)
Async XLA Ops:
  0.6 7.6 %collective-permute-start = (bf16[256,256]{1,0:T(8,128)(2,1)}, bf16[256,256]{1,0:T(8,128)(2,1)S(1)}, u32[]{:S(2)}, u32[]{:S(2)}) collective-permute-start(bf16[256,256]{1,0:T(8,128)(2,1)} %refs_4_.3), channel_id=1, source_target_pairs={{0,16},{16,0},{1,17},{17,1},{2,18},{18,2},{3,19},{19,3},{4,20},{20... | collective-permute-start | bytes 393224 | tf_op jit(solution)/shard_map/ppermute | solution.py:384
  4.9 6.5 %collective-permute-start.1 = (bf16[256,256]{1,0:T(8,128)(2,1)}, bf16[256,256]{1,0:T(8,128)(2,1)S(1)}, u32[]{:S(2)}, u32[]{:S(2)}) collective-permute-start(bf16[256,256]{1,0:T(8,128)(2,1)} %refs_5_.3), channel_id=1, source_target_pairs={{0,16},{16,0},{1,17},{17,1},{2,18},{18,2},{3,19},{19,3},{4,20},{20... | collective-permute-start | bytes 393224 | tf_op jit(solution)/shard_map/ppermute | solution.py:384
  9.4 6.2 %collective-permute-start.2 = (bf16[256,256]{1,0:T(8,128)(2,1)S(1)}, bf16[256,256]{1,0:T(8,128)(2,1)S(1)}, u32[]{:S(2)}, u32[]{:S(2)}) collective-permute-start(bf16[256,256]{1,0:T(8,128)(2,1)S(1)} %bitcast.3), channel_id=1, source_target_pairs={{0,16},{16,0},{1,17},{17,1},{2,18},{18,2},{3,19},{19,3},{4,20},{20... | collective-permute-start | bytes 393224 | tf_op jit(solution)/shard_map/ppermute | solution.py:384
  12.5 5.4 %collective-permute-start.3 = (bf16[256,256]{1,0:T(8,128)(2,1)S(1)}, bf16[256,256]{1,0:T(8,128)(2,1)S(1)}, u32[]{:S(2)}, u32[]{:S(2)}) collective-permute-start(bf16[256,256]{1,0:T(8,128)(2,1)S(1)} %bitcast.4), channel_id=1, source_target_pairs={{0,16},{16,0},{1,17},{17,1},{2,18},{18,2},{3,19},{19,3},{4,20},{20... | collective-permute-start | bytes 393224 | tf_op jit(solution)/shard_map/ppermute | solution.py:384

commit v3 on v0

--- a/solution.py
+++ b/solution.py
@@ -42,19 +42,6 @@
             return carry
 
         lax.fori_loop(0, steps, one, 0)
-
-
-def added(steps, unroll, step, total_ref):
-    if unroll:
-        return functools.reduce(jnp.add, [step(i) for i in range(steps)])
-    (total_ref,) = total_ref
-    total_ref[...] = jnp.zeros_like(total_ref)
-
-    def one(i):
-        total_ref[...] += step(i)
-
-    repeat(steps, unroll, one)
-    return total_ref[...]
 
 
 def columns(i, width):
@@ -240,7 +227,7 @@
 
 
 def far_key_kernel(
-    unroll, q_ref, g_ref, k_ref, stats_ref, table_ref, back_ref, p_ref, fin_ref, *total_ref
+    unroll, q_ref, g_ref, k_ref, stats_ref, table_ref, back_ref, p_ref, fin_ref
 ):
     far_tiles = k_ref.shape[0] // TILE
     heads = k_ref.shape[1] // WIDTH
@@ -261,11 +248,10 @@
             fade = jnp.exp2(near_top - top)
             inverse = 1.0 / (stats_ref[1:2, at] * fade + jnp.sum(p, axis=0, keepdims=True))
             fin_ref[0:1, at] = fade * inverse
-            p = (p * inverse).astype(BF16)
-            p_ref[head, :, here] = p
-            return dot_nn(p, pair_rows(g_ref, pair))
-
-        dv = added(per_head, unroll, step, total_ref).astype(BF16)
+            p_ref[head, :, here] = (p * inverse).astype(BF16)
+
+        repeat(per_head, unroll, step)
+        dv = dot_nn(p_ref[head], stacked_rows(g_ref, head, 2 * per_head)).astype(BF16)
         for shift in range(shifts):
             back_ref[shift, :, cols] = dv[shift * own_keys : (shift + 1) * own_keys]
 
@@ -273,7 +259,7 @@
 def far_value_kernel(
     unroll, q_ref, g_ref, v_ref, p_ref, fin_ref, near_v_ref, near_p_ref, *refs
 ):
-    d_ref, stats_ref, back_ref, ds_ref, delta_ref, *total_ref = refs[2:]
+    d_ref, stats_ref, back_ref, ds_ref, delta_ref = refs[2:]
     heads = v_ref.shape[1] // WIDTH
     per_head = q_ref.shape[1] // PAIR // heads
     shifts, own_keys, _ = back_ref.shape
@@ -293,11 +279,10 @@
             p = p_ref[head, :, here].astype(F32)
             delta = stats_ref[2:3, at] * fin_ref[0:1, at] + jnp.sum(p * d, axis=0, keepdims=True)
             delta_ref[0:1, at] = delta
-            ds = (p * (d - delta)).astype(BF16)
-            ds_ref[head, :, here] = ds
-            return dot_nn(ds, pair_rows(q_ref, pair))
-
-        dk = (added(per_head, unroll, step, total_ref) * SCALE).astype(BF16)
+            ds_ref[head, :, here] = (p * (d - delta)).astype(BF16)
+
+        repeat(per_head, unroll, step)
+        dk = (dot_nn(ds_ref[head], stacked_rows(q_ref, head, 2 * per_head)) * SCALE).astype(BF16)
         for shift in range(shifts):
             back_ref[shift, :, cols] = dk[shift * own_keys : (shift + 1) * own_keys]
 
@@ -417,7 +402,6 @@
         aliases={len(here) + 1 + i: i for i in range(NEAR_OUTS)},
     )
     mib = 32 if unroll else 60
-    total = [] if unroll else [pltpu.VMEM((far_keys, WIDTH), F32)]
     far_k = far_k[0] if ctx == 2 else jnp.concatenate(far_k, axis=0)
     back_v, far_p, fin = call(
         functools.partial(far_key_kernel, unroll),
@@ -427,7 +411,7 @@
             shape((heads, far_keys, group_rows), BF16),
             shape((8, heads * group_rows), F32),
         ],
-        total,
+        [],
         2 * product * far_keys // WIDTH,
         mib,
         q, g, far_k, stats, table,
@@ -445,7 +429,7 @@
             shape((heads, far_keys, group_rows), BF16),
             shape((8, heads * group_rows), F32),
         ],
-        total,
+        [],
         2 * product * far_keys // WIDTH,
         mib,
         q, g, far_v, far_p, fin, near_v, near_p, near_d, stats,

time: 18.1 us -> 18.4 us (1.017)
  Pallas kernels: 9.45 us -> 9.92 us
  starting transfers between devices: 6.66 us -> 6.37 us
    pallas_call x7, Pallas kernels: 9.45 us -> 9.92 us  [call(): pl.pallas_call(kernel, out_shape=outs, in_specs=[pl.BlockSpec(memory_spac...]
    ppermute x4, starting transfers between devices: 6.66 us -> 6.37 us  [shifted(): return lax.ppermute(x, 'ctx', [(o, (o - shift) % ctx) for o in range(ctx)])]
  transfers between devices with their start and end apart: 4 -> 4, of which waited for: 1 -> 1; matrix products, arithmetic and copies ran while one was open for 0% -> 0% of each run, Pallas kernels for 49% -> 51%
where the time goes in v3:
time: 18.4 us; the launch traced here: 18.2 us
  Pallas kernels  9.92 us (54%)
  starting transfers between devices  6.37 us (35%)
  between operations  1.31 us (7%)
  waiting for transfers between devices  0.62 us (3%)
    pallas_call x7, Pallas kernels, call(): pl.pallas_call(kernel, out_shape=outs, in_specs=[pl.BlockSpec(memory_spac...  9.92 us
    ppermute x4, starting transfers between devices, shifted(): return lax.ppermute(x, 'ctx', [(o, (o - shift) % ctx) for o in range(ctx)])  6.37 us
    ppermute x4, waiting for transfers between devices, shifted(): return lax.ppermute(x, 'ctx', [(o, (o - shift) % ctx) for o in range(ctx)])  0.62 us
  transfers between devices with their start and end apart: 4, of which 1 were waited for; matrix products, arithmetic and copies ran while one was open for 0% of the time, Pallas kernels for 51%

profile of v3, /device:TPU:0, one launch (start us, length us, event | category | flops | bytes accessed | tf_op | source)
XLA Modules:
  0.0 18.2 jit_solution(13358729680512793020)
XLA Ops:
  0.6 3.0 %collective-permute-start.1 = (bf16[256,256]{1,0:T(8,128)(2,1)}, bf16[256,256]{1,0:T(8,128)(2,1)S(1)}, u32[]{:S(2)}, u32[]{:S(2)}) collective-permute-start(bf16[256,256]{1,0:T(8,128)(2,1)} %refs_4_.3), channel_id=1, source_target_pairs={{0,16},{16,0},{1,17},{17,1},{2,18},{18,2},{3,19},{19,3},{4,20},{20... | collective-permute-start | bytes 393224 | tf_op jit(solution)/shard_map/ppermute | solution.py:361
  3.6 0.1 shard_map.146
  3.7 0.1 collective-permute-start
  4.5 3.3 %shard_map.147 = (bf16[128,2048]{1,0:T(8,128)(2,1)S(1)}, bf16[128,2048]{1,0:T(8,128)(2,1)S(1)}, bf16[384,256]{1,0:T(8,128)(2,1)S(1)}, bf16[384,256]{1,0:T(8,128)...) custom-call(bf16[128,2048]{1,0:T(8,128)(2,1)} %refs_0_.3, ...), custom_call_target="tpu_custom_call", output_to_operand_aliasing={{0}: (11, {}), {1}: (12, {}), {2}: (13, {}), {3}: (14, {}),... | custom-call | flops 201326592 | bytes 17049956 | tf_op jit(solution)/shard_map/pallas_call | solution.py:334
  7.8 0.0 collective-permute-done.1.k_ref.fk_ref
  7.8 1.4 %shard_map.148 = (bf16[1,256,256]{2,1,0:T(8,128)(2,1)S(1)}, bf16[2,256,1024]{2,1,0:T(8,128)(2,1)S(1)}, f32[8,2048]{1,0:T(8,128)S(1)}) custom-call(bf16[128,2048]{1,0:T(8,128)(2,1)S(1)} %get-tuple-element.52.q_ref, bf16[128,2048]{1,0:T(8,128)(2,1)S(1)} %get-tuple-element.53.g_ref, bf16[256,256]{1,0:T(8,128)(2,1)S(1)} %collective-permute-done.1.k_ref.fk_ref, ...), custom_call_target="tpu_custom_call" | custom-call | flops 268435456 | bytes 2494464 | tf_op jit(solution)/shard_map/pallas_call | solution.py:334
  9.3 1.5 %collective-permute-start.2 = (bf16[256,256]{1,0:T(8,128)(2,1)S(1)}, bf16[256,256]{1,0:T(8,128)(2,1)S(1)}, u32[]{:S(2)}, u32[]{:S(2)}) collective-permute-start(bf16[256,256]{1,0:T(8,128)(2,1)S(1)} %bitcast.3), channel_id=1, source_target_pairs={{0,16},{16,0},{1,17},{17,1},{2,18},{18,2},{3,19},{19,3},{4,20},{20... | collective-permute-start | bytes 393224 | tf_op jit(solution)/shard_map/ppermute | solution.py:361
  10.7 0.0 collective-permute-done.v_ref
  10.8 1.3 %shard_map.149 = (f32[2,384,1024]{2,1,0:T(8,128)S(1)}, f32[8,2048]{1,0:T(8,128)S(1)}, bf16[1,256,256]{2,1,0:T(8,128)(2,1)S(1)}, bf16[2,256,1024]{2,1,0:T(8,128)(2,1)S(1)}, f32[8,2048]{1,0:T(8,128)S(1)}) custom-call(bf16[128,2048]{1,0:T(8,128)(2,1)S(1)} %get-tuple-element.52.q_ref, ...), custom_call_target="tpu_custom_call", output_to_operand_aliasing={{0}: (7, {}), {1}: (8, {})} | custom-call | flops 268435456 | bytes 13303808 | tf_op jit(solution)/shard_map/pallas_call | solution.py:334
  12.1 1.8 %collective-permute-start.3 = (bf16[256,256]{1,0:T(8,128)(2,1)S(1)}, bf16[256,256]{1,0:T(8,128)(2,1)S(1)}, u32[]{:S(2)}, u32[]{:S(2)}) collective-permute-start(bf16[256,256]{1,0:T(8,128)(2,1)S(1)} %bitcast.4), channel_id=1, source_target_pairs={{0,16},{16,0},{1,17},{17,1},{2,18},{18,2},{3,19},{19,3},{4,20},{20... | collective-permute-start | bytes 393224 | tf_op jit(solution)/shard_map/ppermute | solution.py:361
  13.9 2.3 %shard_map.150 = (bf16[128,2048]{1,0:T(8,128)(2,1)}, bf16[128,256]{1,0:T(8,128)(2,1)}, bf16[128,256]{1,0:T(8,128)(2,1)}, f32[256,256]{1,0:T(8,128)S(1)}, f32[256,256]{1,0:T(8,128)S(1)}) custom-call(bf16[128,2048]{1,0:T(8,128)(2,1)S(1)} %get-tuple-element.52.q_ref, bf16[128,2048]{1,0:T(8,128)(2,1)S(1)} %get-tuple-element.53.g_ref, ...), custom_call_target="tpu_custom_call" | custom-call | flops 738197504 | bytes 10027008 | tf_op jit(solution)/shard_map/pallas_call | solution.py:334
  16.2 0.0 collective-permute-done.2.refs_0_
  16.2 0.7 %shard_map.151.after_ref = f32[256,256]{1,0:T(8,128)} custom-call(bf16[128,2048]{1,0:T(8,128)(2,1)} %get-tuple-element.34.after_ref, f32[256,256]{1,0:T(8,128)S(1)} %get-tuple-element.69.own_ref, bf16[256,256]{1,0:T(8,128)(2,1)S(1)} %collective-permute-done.2.refs_0_), custom_call_target="tpu_custom_call" | custom-call | bytes 1179648 | tf_op jit(solution)/shard_map/pallas_call | solution.py:334
  16.9 0.6 %collective-permute-done.3.refs_0_ = bf16[256,256]{1,0:T(8,128)(2,1)S(1)} collective-permute-done((bf16[256,256]{1,0:T(8,128)(2,1)S(1)}, bf16[256,256]{1,0:T(8,128)(2,1)S(1)}, u32[]{:S(2)}, u32[]{:S(2)}) %collective-permute-start.3) | collective-permute-done | bytes 131104 | tf_op jit(solution)/shard_map/ppermute | solution.py:361
  17.5 0.7 %shard_map.152 = f32[256,256]{1,0:T(8,128)} custom-call(f32[256,256]{1,0:T(8,128)} %shard_map.151.after_ref, f32[256,256]{1,0:T(8,128)S(1)} %get-tuple-element.71.own_ref, bf16[256,256]{1,0:T(8,128)(2,1)S(1)} %collective-permute-done.3.refs_0_), custom_call_target="tpu_custom_call" | custom-call | bytes 917504 | tf_op jit(solution)/shard_map/pallas_call | solution.py:334
Async XLA Ops:
  0.6 7.2 %collective-permute-start.1 = (bf16[256,256]{1,0:T(8,128)(2,1)}, bf16[256,256]{1,0:T(8,128)(2,1)S(1)}, u32[]{:S(2)}, u32[]{:S(2)}) collective-permute-start(bf16[256,256]{1,0:T(8,128)(2,1)} %refs_4_.3), channel_id=1, source_target_pairs={{0,16},{16,0},{1,17},{17,1},{2,18},{18,2},{3,19},{19,3},{4,20},{20... | collective-permute-start | bytes 393224 | tf_op jit(solution)/shard_map/ppermute | solution.py:361
  3.7 7.0 %collective-permute-start = (bf16[256,256]{1,0:T(8,128)(2,1)}, bf16[256,256]{1,0:T(8,128)(2,1)S(1)}, u32[]{:S(2)}, u32[]{:S(2)}) collective-permute-start(bf16[256,256]{1,0:T(8,128)(2,1)} %refs_5_.3), channel_id=1, source_target_pairs={{0,16},{16,0},{1,17},{17,1},{2,18},{18,2},{3,19},{19,3},{4,20},{20... | collective-permute-start | bytes 393224 | tf_op jit(solution)/shard_map/ppermute | solution.py:361
  9.3 6.9 %collective-permute-start.2 = (bf16[256,256]{1,0:T(8,128)(2,1)S(1)}, bf16[256,256]{1,0:T(8,128)(2,1)S(1)}, u32[]{:S(2)}, u32[]{:S(2)}) collective-permute-start(bf16[256,256]{1,0:T(8,128)(2,1)S(1)} %bitcast.3), channel_id=1, source_target_pairs={{0,16},{16,0},{1,17},{17,1},{2,18},{18,2},{3,19},{19,3},{4,20},{20... | collective-permute-start | bytes 393224 | tf_op jit(solution)/shard_map/ppermute | solution.py:361
  12.1 5.4 %collective-permute-start.3 = (bf16[256,256]{1,0:T(8,128)(2,1)S(1)}, bf16[256,256]{1,0:T(8,128)(2,1)S(1)}, u32[]{:S(2)}, u32[]{:S(2)}) collective-permute-start(bf16[256,256]{1,0:T(8,128)(2,1)S(1)} %bitcast.4), channel_id=1, source_target_pairs={{0,16},{16,0},{1,17},{17,1},{2,18},{18,2},{3,19},{19,3},{4,20},{20... | collective-permute-start | bytes 393224 | tf_op jit(solution)/shard_map/ppermute | solution.py:361
